TPU v7x, 32 devices: a whole 2x2x4 slice. The times are simulated.
32 devices in a mesh: groups: 2 (over y), wide: 8 (over z, x), narrow: 2 (over core).
Axes of the slice: x: 2, y: 2, z: 4, core: 2. Of those that a mesh axis runs over, the one named last changes fastest.
Arguments:
- inputs: bfloat16 [8192, 1024], P(('groups', 'wide', 'narrow')), parts along dimension 0, may hold values from -6 to 6
- filter_taps: bfloat16 [4096, 1024], P(('wide', 'narrow')), may hold values from -6 to 6
- grad_out: bfloat16 [8192, 1024], P(('groups', 'wide', 'narrow')), parts along dimension 0, may hold values from -6 to 6
Outputs:
- outputs: bfloat16 [8192, 1024], P(('groups', 'wide', 'narrow')), parts along dimension 0
- grad_inputs: bfloat16 [8192, 1024], P(('groups', 'wide', 'narrow')), parts along dimension 0
- grad_taps: bfloat16 [8192, 1024], P(('groups', 'wide', 'narrow')), parts along dimension 0
There are 2 independent parts, one for each index of `groups`. A program takes and returns all parts, laid end to end along the dimension named above; an argument that names none is the same for every part. Nothing has to cross between parts.
All inputs are finite; a program needn't handle non-finite values.
Results may differ from a plain program's by a relative error of at most 0.008.
Values may be sent and summed in bfloat16 or wider, within the bound.
A program may use at most 64 MiB of HBM per device.

v0:
```python
import math
import jax
import jax.numpy as jnp
from jax import lax
from jax.sharding import PartitionSpec as P


def partner_2(value, axis, distance):
    mask = 2**distance
    pairs = [(source, source ^ mask) for source in range(lax.axis_size(axis))]
    return lax.ppermute(value, axis, pairs)


def on_device(inputs, filter_taps, grad_out):
    span_count = lax.axis_size("wide")
    blocksize = inputs.shape[0]
    channels = inputs.shape[1]
    shares = channels // span_count
    row_count = span_count * shares
    seq_len = span_count * 2 * blocksize
    parity = lax.axis_index("narrow")
    signed = (1 - 2 * parity).astype(jnp.float32)
    counter = jnp.arange(span_count, dtype=jnp.int32)
    long_angles = (counter[:, None] * counter[None, :] % span_count).astype(jnp.float32) * (
        2.0 * math.pi / span_count
    )
    long_cos = jnp.cos(long_angles)
    long_sin = jnp.sin(long_angles)
    long_forward = jnp.concatenate([long_cos, -long_sin], axis=0).astype(jnp.bfloat16)
    long_inverse = jnp.concatenate([long_cos, -long_sin], axis=1).astype(jnp.bfloat16)
    positions = jnp.arange(blocksize, dtype=jnp.int32)

    def first_section(pieces, twist_cos, twist_sin):
        share_count = pieces.shape[1]
        lane_count = pieces.shape[2]
        flatten = pieces.reshape(span_count, share_count * lane_count)
        mixture = jnp.dot(long_forward, flatten, preferred_element_type=jnp.float32)
        mixture = mixture.reshape(2, span_count, share_count, lane_count)
        real_part = mixture[0] * twist_cos + mixture[1] * twist_sin
        imag_part = mixture[1] * twist_cos - mixture[0] * twist_sin
        return jnp.stack([real_part, imag_part]).astype(jnp.bfloat16)

    def long_back(combined_re, combined_im, twist_cos, twist_sin):
        merged_re = combined_re * twist_cos - combined_im * twist_sin
        merged_im = combined_im * twist_cos + combined_re * twist_sin
        share_count = combined_re.shape[1]
        lane_count = combined_re.shape[2]
        stacked = (
            jnp.stack([merged_re, merged_im])
            .astype(jnp.bfloat16)
            .reshape(2 * span_count, share_count * lane_count)
        )
        summed = jnp.dot(long_inverse, stacked, preferred_element_type=jnp.float32) * (
            1.0 / seq_len
        )
        return summed.astype(jnp.bfloat16).reshape(span_count, share_count, lane_count)

    block_product = positions[:, None] * (2 * positions[None, :] + parity) % (2 * blocksize)
    block_angles = block_product.astype(jnp.float32) * (math.pi / blocksize)
    block_cos = jnp.cos(block_angles)
    block_sin = jnp.sin(block_angles)
    forward_mat = jnp.concatenate(
        [
            jnp.concatenate([block_cos, -block_sin], axis=1),
            jnp.concatenate([block_sin, block_cos], axis=1),
        ],
        axis=0,
    ).astype(jnp.bfloat16)
    cos_turned = jnp.transpose(block_cos)
    sin_turned = jnp.transpose(block_sin)
    inverse_mat = jnp.concatenate(
        [
            jnp.concatenate([cos_turned, sin_turned], axis=1),
            jnp.concatenate([-sin_turned, cos_turned], axis=1),
        ],
        axis=0,
    ).astype(jnp.bfloat16)
    twist_product = (parity * blocksize + positions)[None, None, :] * counter[:, None, None]
    twist_angles = twist_product.astype(jnp.float32) * (2.0 * math.pi / seq_len)
    twist_cos = jnp.cos(twist_angles)
    twist_sin = jnp.sin(twist_angles)

    def section_pairs(pieces):
        return first_section(pieces, twist_cos, twist_sin)

    def spectrum(signal):
        arranged = jnp.transpose(signal).reshape(span_count, shares, blocksize)
        twisted = section_pairs(
            lax.all_to_all(arranged, "wide", split_axis=0, concat_axis=0, tiled=True)
        )
        partner = partner_2(twisted, "narrow", 0)
        paired = (signed * twisted.astype(jnp.float32) + partner.astype(jnp.float32)).astype(
            jnp.bfloat16
        )
        joined = jnp.concatenate(
            [paired[0].reshape(row_count, blocksize), paired[1].reshape(row_count, blocksize)],
            axis=1,
        )
        return jnp.dot(joined, forward_mat, preferred_element_type=jnp.float32)

    def invert(spectrum_in):
        unfolded = jnp.dot(spectrum_in, inverse_mat, preferred_element_type=jnp.float32).astype(
            jnp.bfloat16
        )
        partner = partner_2(unfolded, "narrow", 0)
        combined = signed * unfolded.astype(jnp.float32) + partner.astype(jnp.float32)
        comb_re = combined[:, :blocksize].reshape(span_count, shares, blocksize)
        comb_im = combined[:, blocksize:].reshape(span_count, shares, blocksize)
        arranged = long_back(comb_re, comb_im, twist_cos, twist_sin)
        returned = lax.all_to_all(arranged, "wide", split_axis=0, concat_axis=1, tiled=True)
        return jnp.transpose(returned.reshape(channels, blocksize))

    def product(left_side, right_side, conjugate, factor):
        left_re = left_side[..., :blocksize]
        left_im = left_side[..., blocksize:]
        right_re = right_side[..., :blocksize]
        right_im = right_side[..., blocksize:]
        if conjugate:
            real_part = left_re * right_re + left_im * right_im
            imag_part = left_re * right_im - left_im * right_re
        else:
            real_part = left_re * right_re - left_im * right_im
            imag_part = left_re * right_im + left_im * right_re
        return (jnp.concatenate([real_part, imag_part], axis=-1) * factor).astype(jnp.bfloat16)

    kernel_scale = 1.0 / math.sqrt(seq_len)
    input_spectrum = spectrum(inputs)
    kernel_spectrum = spectrum(filter_taps) * kernel_scale
    outputs = invert(product(kernel_spectrum, input_spectrum, False, 1.0))
    grad_spectrum = spectrum(grad_out)
    grad_inputs = invert(product(kernel_spectrum, grad_spectrum, True, 1.0))
    grad_taps = invert(product(input_spectrum, grad_spectrum, True, kernel_scale))
    return (outputs, grad_inputs, grad_taps)


def solution(mesh):
    in_specs = (
        P(("groups", "wide", "narrow"), None),
        P(("wide", "narrow"), None),
        P(("groups", "wide", "narrow"), None),
    )
    out_specs = (
        P(("groups", "wide", "narrow"), None),
        P(("groups", "wide", "narrow"), None),
        P(("groups", "wide", "narrow"), None),
    )
    return jax.shard_map(
        on_device, mesh=mesh, in_specs=in_specs, out_specs=out_specs, check_vma=False
    )
```

profile of v0, /device:TPU:0, one launch (start us, length us, event | category | flops | bytes accessed | tf_op | source)
XLA Modules:
  0.0 144.9 jit_solution(16948435035127631216)
XLA Ops:
  0.7 2.1 %copy.61 = bf16[1024,256]{1,0:T(8,128)(2,1)} copy(bf16[1024,256]{0,1:T(8,128)(2,1)} %bitcast.84) | data formatting | bytes 1048576 | tf_op jit(solution)/shard_map/reshape | solution.py:87
  2.8 7.3 %all-to-all-start.1 = ((bf16[8,128,256]{2,1,0:T(8,128)(2,1)}), bf16[8,128,256]{2,1,0:T(8,128)(2,1)S(1)}, u32[]{:S(2)}, u32[]{:S(2)}) async-start(bf16[8,128,256]{2,1,0:T(8,128)(2,1)} %bitcast.7), calls=%async_computation.1 | async-start | bytes 1048576 | tf_op jit(solution)/shard_map/all_to_all | solution.py:89
  11.0 13.5 %all-to-all-done.1 = bf16[8,128,256]{2,1,0:T(8,128)(2,1)S(1)} async-done(((bf16[8,128,256]{2,1,0:T(8,128)(2,1)}), bf16[8,128,256]{2,1,0:T(8,128)(2,1)S(1)}, u32[]{:S(2)}, u32[]{:S(2)}) %all-to-all-start.1) | async-done | bytes 524320 | tf_op jit(solution)/shard_map/all_to_all | solution.py:89
  24.5 3.6 %all-to-all-start = ((bf16[8,128,256]{2,1,0:T(8,128)(2,1)}), bf16[8,128,256]{2,1,0:T(8,128)(2,1)S(1)}, u32[]{:S(2)}, u32[]{:S(2)}) async-start(bf16[8,128,256]{2,1,0:T(8,128)(2,1)} %bitcast.1), calls=%async_computation | async-start | bytes 1048576 | tf_op jit(solution)/shard_map/all_to_all | solution.py:89
  29.2 13.7 %all-to-all-done = bf16[8,128,256]{2,1,0:T(8,128)(2,1)S(1)} async-done(((bf16[8,128,256]{2,1,0:T(8,128)(2,1)}), bf16[8,128,256]{2,1,0:T(8,128)(2,1)S(1)}, u32[]{:S(2)}, u32[]{:S(2)}) %all-to-all-start) | async-done | bytes 524320 | tf_op jit(solution)/shard_map/all_to_all | solution.py:89
  42.8 3.6 %all-to-all-start.3 = ((bf16[8,128,256]{2,1,0:T(8,128)(2,1)}), bf16[8,128,256]{2,1,0:T(8,128)(2,1)S(1)}, u32[]{:S(2)}, u32[]{:S(2)}) async-start(bf16[8,128,256]{2,1,0:T(8,128)(2,1)} %bitcast.18), calls=%async_computation.3 | async-start | bytes 1048576 | tf_op jit(solution)/shard_map/all_to_all | solution.py:89
  47.2 13.9 %all-to-all-done.3 = bf16[8,128,256]{2,1,0:T(8,128)(2,1)S(1)} async-done(((bf16[8,128,256]{2,1,0:T(8,128)(2,1)}), bf16[8,128,256]{2,1,0:T(8,128)(2,1)S(1)}, u32[]{:S(2)}, u32[]{:S(2)}) %all-to-all-start.3) | async-done | bytes 524320 | tf_op jit(solution)/shard_map/all_to_all | solution.py:89
  63.1 2.8 %add_convert_fusion.6 = (bf16[1,8,128,256]{3,2,1,0:T(8,128)(2,1)S(1)}, bf16[1,8,128,256]{3,2,1,0:T(8,128)(2,1)S(1)}, bf16[1,8,128,256]{3,2,1,0:T(8,128)(2,1)S(1)...) fusion(f32[1,8,128,256]{3,1,2,0:T(8,128)S(1)} %bitcast.62, ...), kind=kLoop, calls=%fused_computation.50 | loop fusion | flops 6291456 | bytes 9453568 | tf_op jit(solution)/shard_map/convert.6
  65.9 1.1 pad_maximum_fusion
  66.9 1.1 pad_maximum_fusion.1
  68.5 2.5 %fusion.36 = (bf16[256,256]{1,0:T(8,128)(2,1)S(1)}, bf16[256,256]{1,0:T(8,128)(2,1)S(1)}, bf16[256,256]{1,0:T(8,128)(2,1)S(1)}, bf16[256,256]{1,0:T(8,128)(2,1)S...) fusion(s32[256]{0:T(256)S(1)} %multiply_add_fusion.1), kind=kLoop, calls=%fused_computation.85 | loop fusion | flops 2359296 | bytes 787456 | tf_op jit(solution)/shard_map/convert.15
  71.2 1.5 %add_convert_fusion.2 = bf16[2,8,128,256]{3,2,1,0:T(8,128)(2,1)S(1)} fusion(bf16[2,8,128,256]{3,2,1,0:T(8,128)(2,1)} %collective-permute-done, f32[]{:T(128)S(6)} %convert_element_type.121, bf16[1,8,128,256]{3,2,1,0:T(8,128)(2,1)S(1)} %get-tuple-element.47, bf16[1,8,128,256]{3,2,1,0:T(8,128)(2,1)S(1)} %get-tuple-element.48), kind=kLoop, calls=%fused_computation.13 | loop fusion | flops 3145728 | bytes 3145732 | tf_op jit(solution)/shard_map/convert_element_type | solution.py:92
  72.9 1.5 %add_convert_fusion.1 = bf16[2,8,128,256]{3,2,1,0:T(8,128)(2,1)S(1)} fusion(bf16[2,8,128,256]{3,2,1,0:T(8,128)(2,1)} %collective-permute-done.1, f32[]{:T(128)S(6)} %convert_element_type.121, bf16[1,8,128,256]{3,2,1,0:T(8,128)(2,1)S(1)} %get-tuple-element.45, bf16[1,8,128,256]{3,2,1,0:T(8,128)(2,1)S(1)} %get-tuple-element.46), kind=kLoop, calls=%fused_computation.12 | loop fusion | flops 3145728 | bytes 3145732 | tf_op jit(solution)/shard_map/convert_element_type | solution.py:92
  77.3 1.0 multiply_add_fusion
  83.9 1.0 collective-permute-done.4
  85.4 1.1 subtract_convert_fusion
  88.5 3.7 %all-to-all-start.5 = ((bf16[8,128,256]{2,1,0:T(8,128)(2,1)}), bf16[8,128,256]{2,1,0:T(8,128)(2,1)S(1)}, u32[]{:S(2)}, u32[]{:S(2)}) async-start(bf16[8,128,256]{2,1,0:T(8,128)(2,1)} %copy.58), calls=%async_computation.5 | async-start | bytes 1048576 | tf_op jit(solution)/shard_map/all_to_all | solution.py:110
  94.1 13.1 %all-to-all-done.5 = bf16[8,128,256]{2,1,0:T(8,128)(2,1)S(1)} async-done(((bf16[8,128,256]{2,1,0:T(8,128)(2,1)}), bf16[8,128,256]{2,1,0:T(8,128)(2,1)S(1)}, u32[]{:S(2)}, u32[]{:S(2)}) %all-to-all-start.5) | async-done | bytes 524320 | tf_op jit(solution)/shard_map/all_to_all | solution.py:110
  107.2 3.6 %all-to-all-start.2 = ((bf16[8,128,256]{2,1,0:T(8,128)(2,1)}), bf16[8,128,256]{2,1,0:T(8,128)(2,1)S(1)}, u32[]{:S(2)}, u32[]{:S(2)}) async-start(bf16[8,128,256]{2,1,0:T(8,128)(2,1)} %copy.49), calls=%async_computation.2 | async-start | bytes 1048576 | tf_op jit(solution)/shard_map/all_to_all | solution.py:110
  112.8 12.7 %all-to-all-done.2 = bf16[8,128,256]{2,1,0:T(8,128)(2,1)S(1)} async-done(((bf16[8,128,256]{2,1,0:T(8,128)(2,1)}), bf16[8,128,256]{2,1,0:T(8,128)(2,1)S(1)}, u32[]{:S(2)}, u32[]{:S(2)}) %all-to-all-start.2) | async-done | bytes 524320 | tf_op jit(solution)/shard_map/all_to_all | solution.py:110
  125.5 3.6 %all-to-all-start.4 = ((bf16[8,128,256]{2,1,0:T(8,128)(2,1)}), bf16[8,128,256]{2,1,0:T(8,128)(2,1)S(1)}, u32[]{:S(2)}, u32[]{:S(2)}) async-start(bf16[8,128,256]{2,1,0:T(8,128)(2,1)} %copy.56), calls=%async_computation.4 | async-start | bytes 1048576 | tf_op jit(solution)/shard_map/all_to_all | solution.py:110
  129.2 1.0 copy.59
  131.2 12.7 %all-to-all-done.4 = bf16[8,128,256]{2,1,0:T(8,128)(2,1)S(1)} async-done(((bf16[8,128,256]{2,1,0:T(8,128)(2,1)}), bf16[8,128,256]{2,1,0:T(8,128)(2,1)S(1)}, u32[]{:S(2)}, u32[]{:S(2)}) %all-to-all-start.4) | async-done | bytes 524320 | tf_op jit(solution)/shard_map/all_to_all | solution.py:110
  143.9 1.0 copy.57
  (61 shorter events, 21.0 us)
Async XLA Ops:
  0.6 9.4 %copy-start = (bf16[256,1024]{1,0:T(8,128)(2,1)S(1)}, bf16[256,1024]{1,0:T(8,128)(2,1)}, u32[]{:S(2)}) copy-start(bf16[256,1024]{1,0:T(8,128)(2,1)} %param.4) | copy-start | bytes 1572868
  0.6 27.5 %copy-start.1 = (bf16[256,1024]{1,0:T(8,128)(2,1)S(1)}, bf16[256,1024]{1,0:T(8,128)(2,1)}, u32[]{:S(2)}) copy-start(bf16[256,1024]{1,0:T(8,128)(2,1)} %param.5) | copy-start | bytes 1572868
  2.8 21.7 %all-to-all-start.1 = ((bf16[8,128,256]{2,1,0:T(8,128)(2,1)}), bf16[8,128,256]{2,1,0:T(8,128)(2,1)S(1)}, u32[]{:S(2)}, u32[]{:S(2)}) async-start(bf16[8,128,256]{2,1,0:T(8,128)(2,1)} %bitcast.7), calls=%async_computation.1 | async-start | bytes 1048576 | tf_op jit(solution)/shard_map/all_to_all | solution.py:89
  24.5 18.3 %all-to-all-start = ((bf16[8,128,256]{2,1,0:T(8,128)(2,1)}), bf16[8,128,256]{2,1,0:T(8,128)(2,1)S(1)}, u32[]{:S(2)}, u32[]{:S(2)}) async-start(bf16[8,128,256]{2,1,0:T(8,128)(2,1)} %bitcast.1), calls=%async_computation | async-start | bytes 1048576 | tf_op jit(solution)/shard_map/all_to_all | solution.py:89
  42.8 18.3 %all-to-all-start.3 = ((bf16[8,128,256]{2,1,0:T(8,128)(2,1)}), bf16[8,128,256]{2,1,0:T(8,128)(2,1)S(1)}, u32[]{:S(2)}, u32[]{:S(2)}) async-start(bf16[8,128,256]{2,1,0:T(8,128)(2,1)} %bitcast.18), calls=%async_computation.3 | async-start | bytes 1048576 | tf_op jit(solution)/shard_map/all_to_all | solution.py:89
  66.9 4.3 %collective-permute-start = (bf16[2,8,128,256]{3,2,1,0:T(8,128)(2,1)}, bf16[2,8,128,256]{3,2,1,0:T(8,128)(2,1)}, u32[]{:S(2)}, u32[]{:S(2)}) collective-permute-start(bf16[2,8,128,256]{3,2,1,0:T(8,128)(2,1)} %pad_maximum_fusion), channel_id=1, source_target_pairs={{0,1},{1,0},{2,3},{3,2},{4,5},{5,4},{6,7},{7,6},{8,9},{9,8},{10,11... | collective-permute-start | bytes 3145736 | tf_op jit(solution)/shard_map/ppermute | solution.py:11
  68.0 4.9 %collective-permute-start.1 = (bf16[2,8,128,256]{3,2,1,0:T(8,128)(2,1)}, bf16[2,8,128,256]{3,2,1,0:T(8,128)(2,1)}, u32[]{:S(2)}, u32[]{:S(2)}) collective-permute-start(bf16[2,8,128,256]{3,2,1,0:T(8,128)(2,1)} %pad_maximum_fusion.1), channel_id=1, source_target_pairs={{0,1},{1,0},{2,3},{3,2},{4,5},{5,4},{6,7},{7,6},{8,9},{9,8},{10,11... | collective-permute-start | bytes 3145736 | tf_op jit(solution)/shard_map/ppermute | solution.py:11
  71.2 3.4 %collective-permute-start.3 = (bf16[2,8,128,256]{3,2,1,0:T(8,128)(2,1)S(1)}, bf16[2,8,128,256]{3,2,1,0:T(8,128)(2,1)S(1)}, u32[]{:S(2)}, u32[]{:S(2)}) collective-permute-start(bf16[2,8,128,256]{3,2,1,0:T(8,128)(2,1)S(1)} %pad_maximum_fusion.2), channel_id=1, source_target_pairs={{0,1},{1,0},{2,3},{3,2},{4,5},{5,4},{6,7},{7,6},{8,9},{9,8},{10,11... | collective-permute-start | bytes 3145736 | tf_op jit(solution)/shard_map/ppermute | solution.py:11
  79.1 3.2 %collective-permute-start.2 = (bf16[1024,512]{1,0:T(8,128)(2,1)S(1)}, bf16[1024,512]{1,0:T(8,128)(2,1)S(1)}, u32[]{:S(2)}, u32[]{:S(2)}) collective-permute-start(bf16[1024,512]{1,0:T(8,128)(2,1)S(1)} %convolution_convert_fusion.2), channel_id=1, source_target_pairs={{0,1},{1,0},{2,3},{3,2},{4,5},{5,4},{6,7},{7,6},{8,9},{9,8},{10,11... | collective-permute-start | bytes 3145736 | tf_op jit(solution)/shard_map/ppermute | solution.py:11
  80.4 3.0 %collective-permute-start.5 = (bf16[1024,512]{1,0:T(8,128)(2,1)S(1)}, bf16[1024,512]{1,0:T(8,128)(2,1)S(1)}, u32[]{:S(2)}, u32[]{:S(2)}) collective-permute-start(bf16[1024,512]{1,0:T(8,128)(2,1)S(1)} %convolution_convert_fusion), channel_id=1, source_target_pairs={{0,1},{1,0},{2,3},{3,2},{4,5},{5,4},{6,7},{7,6},{8,9},{9,8},{10,11... | collective-permute-start | bytes 3145736 | tf_op jit(solution)/shard_map/ppermute | solution.py:11
  81.8 3.1 %collective-permute-start.4 = (bf16[1024,512]{1,0:T(8,128)(2,1)S(1)}, bf16[1024,512]{1,0:T(8,128)(2,1)S(1)}, u32[]{:S(2)}, u32[]{:S(2)}) collective-permute-start(bf16[1024,512]{1,0:T(8,128)(2,1)S(1)} %convolution_convert_fusion.1), channel_id=1, source_target_pairs={{0,1},{1,0},{2,3},{3,2},{4,5},{5,4},{6,7},{7,6},{8,9},{9,8},{10,11... | collective-permute-start | bytes 3145736 | tf_op jit(solution)/shard_map/ppermute | solution.py:11
  88.5 18.7 %all-to-all-start.5 = ((bf16[8,128,256]{2,1,0:T(8,128)(2,1)}), bf16[8,128,256]{2,1,0:T(8,128)(2,1)S(1)}, u32[]{:S(2)}, u32[]{:S(2)}) async-start(bf16[8,128,256]{2,1,0:T(8,128)(2,1)} %copy.58), calls=%async_computation.5 | async-start | bytes 1048576 | tf_op jit(solution)/shard_map/all_to_all | solution.py:110
  107.2 18.3 %all-to-all-start.2 = ((bf16[8,128,256]{2,1,0:T(8,128)(2,1)}), bf16[8,128,256]{2,1,0:T(8,128)(2,1)S(1)}, u32[]{:S(2)}, u32[]{:S(2)}) async-start(bf16[8,128,256]{2,1,0:T(8,128)(2,1)} %copy.49), calls=%async_computation.2 | async-start | bytes 1048576 | tf_op jit(solution)/shard_map/all_to_all | solution.py:110
  125.5 18.3 %all-to-all-start.4 = ((bf16[8,128,256]{2,1,0:T(8,128)(2,1)}), bf16[8,128,256]{2,1,0:T(8,128)(2,1)S(1)}, u32[]{:S(2)}, u32[]{:S(2)}) async-start(bf16[8,128,256]{2,1,0:T(8,128)(2,1)} %copy.56), calls=%async_computation.4 | async-start | bytes 1048576 | tf_op jit(solution)/shard_map/all_to_all | solution.py:110
where the time goes:
time: 146 us; the launch traced here: 145 us
  waiting for transfers between devices  81.3 us (56%)
  starting transfers between devices  27.2 us (19%)
  other arithmetic  15 us (10%)
  local copies, waits for them, and re-layouts  13.6 us (9%)
  matrix products  6.81 us (5%)
    all_to_all x3, waiting for transfers between devices, spectrum(): lax.all_to_all(arranged, 'wide', split_axis=0, concat_axis=0, tiled=True)  41.1 us
    all_to_all x3, waiting for transfers between devices, invert(): lax.all_to_all(arranged, 'wide', split_axis=0, concat_axis=1, tiled=True)  38.5 us
    all_to_all x3, starting transfers between devices, spectrum(): lax.all_to_all(arranged, 'wide', split_axis=0, concat_axis=0, tiled=True)  14.5 us
    all_to_all x3, starting transfers between devices, invert(): lax.all_to_all(arranged, 'wide', split_axis=0, concat_axis=1, tiled=True)  10.9 us
    another operation x5, other arithmetic  6.97 us
    reshape x3, local copies, waits for them, and re-layouts, spectrum(): arranged = jnp.transpose(signal).reshape(span_count, shares, blocksize)  4.13 us
    convert_element_type x3, other arithmetic, spectrum(): (signed * twisted.astype(jnp.float32) + partner.astype(jnp.float32)).asty...  3.43 us
    reshape x3, local copies, waits for them, and re-layouts, invert(): return jnp.transpose(returned.reshape(channels, blocksize))  3 us
  transfers between devices with their start and end apart: 12, of which 8 were waited for; matrix products, arithmetic and copies ran while one was open for 13% of the time, Pallas kernels for 0%

commit v1 on v0

--- a/solution.py
+++ b/solution.py
@@ -3,6 +3,20 @@
 import jax.numpy as jnp
 from jax import lax
 from jax.sharding import PartitionSpec as P
+
+
+def direct_leaves(z, axis_k, x_in):
+    h_now = z.shape
+    moved = z.reshape(*h_now[:axis_k], x_in, h_now[axis_k] // x_in, *h_now[axis_k + 1 :])
+    return jnp.moveaxis(moved, axis_k, 0)
+
+
+def end_goods(array_here, dimension_no):
+    array_here = jnp.moveaxis(array_here, 0, dimension_no)
+    now = array_here.shape
+    return array_here.reshape(
+        *now[:dimension_no], now[dimension_no] * now[dimension_no + 1], *now[dimension_no + 2 :]
+    )
 
 
 def partner_2(value, axis, distance):
@@ -85,9 +99,22 @@
 
     def spectrum(signal):
         arranged = jnp.transpose(signal).reshape(span_count, shares, blocksize)
-        twisted = section_pairs(
-            lax.all_to_all(arranged, "wide", split_axis=0, concat_axis=0, tiled=True)
-        )
+
+        def use_the_field(vec, peer_axis, original, packet=0):
+            k_now = lax.psum(1, peer_axis)
+            state_next = lax.axis_index(peer_axis)
+            x_new, carry = (k_now, state_next)
+            big = direct_leaves(vec, original, x_new)
+            grid = [big[carry]]
+            for no in range(1, x_new):
+                after = big[carry ^ no]
+                near = lax.ppermute(after, peer_axis, [(j0, j0 ^ no) for j0 in range(x_new)])
+                grid.append(near)
+            e_now = jnp.stack(grid)
+            big = e_now[carry ^ jnp.arange(x_new)]
+            return end_goods(big, packet)
+
+        twisted = section_pairs(use_the_field(arranged, "wide", 0))
         partner = partner_2(twisted, "narrow", 0)
         paired = (signed * twisted.astype(jnp.float32) + partner.astype(jnp.float32)).astype(
             jnp.bfloat16

time: 146 us -> 161 us (1.10)
  starting transfers between devices: 27.2 us -> 52.6 us
  waiting for transfers between devices: 81.3 us -> 67 us
  local copies, waits for them, and re-layouts: 13.6 us -> 18.1 us
    all_to_all x3 -> x0, waiting for transfers between devices: 41.1 us -> none  [spectrum(): lax.all_to_all(arranged, 'wide', split_axis=0, concat_axis=0, tiled=True)]
    ppermute x0 -> x21, starting transfers between devices: none -> 38.4 us  [use_the_field(): lax.ppermute(after, peer_axis, [(j0, j0 ^ no) for j0 in range(x_new)])]
    ppermute x0 -> x21, waiting for transfers between devices: none -> 26.8 us  [use_the_field(): lax.ppermute(after, peer_axis, [(j0, j0 ^ no) for j0 in range(x_new)])]
    all_to_all x3 -> x0, starting transfers between devices: 14.5 us -> none  [spectrum(): lax.all_to_all(arranged, 'wide', split_axis=0, concat_axis=0, tiled=True)]
    reshape x3 -> x0, local copies, waits for them, and re-layouts: 4.13 us -> none  [spectrum(): arranged = jnp.transpose(signal).reshape(span_count, shares, blocksize)]
    unnamed x10 -> x30, local copies, waits for them, and re-layouts: 2.65 us -> 6.11 us
    gather x0 -> x3, local copies, waits for them, and re-layouts: none -> 1.74 us  [use_the_field(): big = e_now[carry ^ jnp.arange(x_new)]]
    transpose x0 -> x3, local copies, waits for them, and re-layouts: none -> 1.73 us  [spectrum(): arranged = jnp.transpose(signal).reshape(span_count, shares, blocksize)]
  transfers between devices with their start and end apart: 12 -> 30, of which waited for: 8 -> 14; matrix products, arithmetic and copies ran while one was open for 13% -> 14% of each run, Pallas kernels for 0% -> 0%
where the time goes in v1:
time: 161 us
  waiting for transfers between devices  67 us (42%)
  starting transfers between devices  52.6 us (33%)
  local copies, waits for them, and re-layouts  18.1 us (11%)
  other arithmetic  14.8 us (9%)
  matrix products  6.81 us (4%)
    all_to_all x3, waiting for transfers between devices, invert(): lax.all_to_all(arranged, 'wide', split_axis=0, concat_axis=1, tiled=True)  38.5 us
    ppermute x21, starting transfers between devices, use_the_field(): lax.ppermute(after, peer_axis, [(j0, j0 ^ no) for j0 in range(x_new)])  38.4 us
    ppermute x21, waiting for transfers between devices, use_the_field(): lax.ppermute(after, peer_axis, [(j0, j0 ^ no) for j0 in range(x_new)])  26.8 us
    all_to_all x3, starting transfers between devices, invert(): lax.all_to_all(arranged, 'wide', split_axis=0, concat_axis=1, tiled=True)  12.4 us
    another operation x5, other arithmetic  6.79 us
    unnamed x30, local copies, waits for them, and re-layouts  6.11 us
    convert_element_type x3, other arithmetic, spectrum(): (signed * twisted.astype(jnp.float32) + partner.astype(jnp.float32)).asty...  3.43 us
  transfers between devices with their start and end apart: 30, of which 14 were waited for; matrix products, arithmetic and copies ran while one was open for 14% of the time, Pallas kernels for 0%

profile of v1, /device:TPU:0, one launch (start us, length us, event | category | flops | bytes accessed | tf_op | source)
XLA Modules:
  0.0 160.5 jit_solution(924927661435250348)
XLA Ops:
  2.8 6.0 %collective-permute-start.14 = (bf16[1,128,256]{2,1,0:T(8,128)(2,1)S(1)}, bf16[1,128,256]{2,1,0:T(8,128)(2,1)}, u32[]{:S(2)}, u32[]{:S(2)}) collective-permute-start(bf16[1,128,256]{2,1,0:T(8,128)(2,1)S(1)} %get-tuple-element.57), channel_id=1, source_target_pairs={{0,14},{2,12},{4,10},{6,8},{8,6},{10,4},{12,2},{14,0},{1,15},{3,13... | collective-permute-start | bytes 196616 | tf_op jit(solution)/shard_map/ppermute | solution.py:111
  14.1 2.4 %collective-permute-done.8 = bf16[1,128,256]{2,1,0:T(8,128)(2,1)} collective-permute-done((bf16[1,128,256]{2,1,0:T(8,128)(2,1)}, bf16[1,128,256]{2,1,0:T(8,128)(2,1)}, u32[]{:S(2)}, u32[]{:S(2)}) %collective-permute-start.8) | collective-permute-done | bytes 65568 | tf_op jit(solution)/shard_map/ppermute | solution.py:111
  18.6 2.3 %collective-permute-done.9 = bf16[1,128,256]{2,1,0:T(8,128)(2,1)S(1)} collective-permute-done((bf16[1,128,256]{2,1,0:T(8,128)(2,1)S(1)}, bf16[1,128,256]{2,1,0:T(8,128)(2,1)S(1)}, u32[]{:S(2)}, u32[]{:S(2)}) %collective-permute-start.9) | collective-permute-done | bytes 65568 | tf_op jit(solution)/shard_map/ppermute | solution.py:111
  20.9 2.0 %collective-permute-start.10 = (bf16[1,128,256]{2,1,0:T(8,128)(2,1)S(1)}, bf16[1,128,256]{2,1,0:T(8,128)(2,1)S(1)}, u32[]{:S(2)}, u32[]{:S(2)}) collective-permute-start(bf16[1,128,256]{2,1,0:T(8,128)(2,1)S(1)} %get-tuple-element.61), channel_id=1, source_target_pairs={{0,6},{2,4},{4,2},{6,0},{8,14},{10,12},{12,10},{14,8},{1,7},{3,5},... | collective-permute-start | bytes 196616 | tf_op jit(solution)/shard_map/ppermute | solution.py:111
  22.9 3.2 %collective-permute-done.10 = bf16[1,128,256]{2,1,0:T(8,128)(2,1)S(1)} collective-permute-done((bf16[1,128,256]{2,1,0:T(8,128)(2,1)S(1)}, bf16[1,128,256]{2,1,0:T(8,128)(2,1)S(1)}, u32[]{:S(2)}, u32[]{:S(2)}) %collective-permute-start.10) | collective-permute-done | bytes 65568 | tf_op jit(solution)/shard_map/ppermute | solution.py:111
  26.1 4.9 %collective-permute-start.6 = (bf16[1,128,256]{2,1,0:T(8,128)(2,1)S(1)}, bf16[1,128,256]{2,1,0:T(8,128)(2,1)S(1)}, u32[]{:S(2)}, u32[]{:S(2)}) collective-permute-start(bf16[1,128,256]{2,1,0:T(8,128)(2,1)S(1)} %get-tuple-element.49), channel_id=1, source_target_pairs={{0,14},{2,12},{4,10},{6,8},{8,6},{10,4},{12,2},{14,0},{1,15},{3,13... | collective-permute-start | bytes 196616 | tf_op jit(solution)/shard_map/ppermute | solution.py:111
  33.3 2.4 %collective-permute-start.3 = (bf16[1,128,256]{2,1,0:T(8,128)(2,1)S(1)}, bf16[1,128,256]{2,1,0:T(8,128)(2,1)S(1)}, u32[]{:S(2)}, u32[]{:S(2)}) collective-permute-start(bf16[1,128,256]{2,1,0:T(8,128)(2,1)S(1)} %get-tuple-element.52), channel_id=1, source_target_pairs={{0,8},{2,10},{4,12},{6,14},{8,0},{10,2},{12,4},{14,6},{1,9},{3,11}... | collective-permute-start | bytes 196616 | tf_op jit(solution)/shard_map/ppermute | solution.py:111
  38.8 2.0 %collective-permute-done = bf16[1,128,256]{2,1,0:T(8,128)(2,1)S(1)} collective-permute-done((bf16[1,128,256]{2,1,0:T(8,128)(2,1)S(1)}, bf16[1,128,256]{2,1,0:T(8,128)(2,1)S(1)}, u32[]{:S(2)}, u32[]{:S(2)}) %collective-permute-start) | collective-permute-done | bytes 65568 | tf_op jit(solution)/shard_map/ppermute | solution.py:111
  42.3 2.8 %collective-permute-done.1 = bf16[1,128,256]{2,1,0:T(8,128)(2,1)S(1)} collective-permute-done((bf16[1,128,256]{2,1,0:T(8,128)(2,1)S(1)}, bf16[1,128,256]{2,1,0:T(8,128)(2,1)S(1)}, u32[]{:S(2)}, u32[]{:S(2)}) %collective-permute-start.1) | collective-permute-done | bytes 65568 | tf_op jit(solution)/shard_map/ppermute | solution.py:111
  45.1 2.3 %collective-permute-start.2 = (bf16[1,128,256]{2,1,0:T(8,128)(2,1)S(1)}, bf16[1,128,256]{2,1,0:T(8,128)(2,1)S(1)}, u32[]{:S(2)}, u32[]{:S(2)}) collective-permute-start(bf16[1,128,256]{2,1,0:T(8,128)(2,1)S(1)} %get-tuple-element.53), channel_id=1, source_target_pairs={{0,6},{2,4},{4,2},{6,0},{8,14},{10,12},{12,10},{14,8},{1,7},{3,5},... | collective-permute-start | bytes 196616 | tf_op jit(solution)/shard_map/ppermute | solution.py:111
  47.4 3.6 %collective-permute-done.2 = bf16[1,128,256]{2,1,0:T(8,128)(2,1)S(1)} collective-permute-done((bf16[1,128,256]{2,1,0:T(8,128)(2,1)S(1)}, bf16[1,128,256]{2,1,0:T(8,128)(2,1)S(1)}, u32[]{:S(2)}, u32[]{:S(2)}) %collective-permute-start.2) | collective-permute-done | bytes 65568 | tf_op jit(solution)/shard_map/ppermute | solution.py:111
  51.0 4.3 %collective-permute-start.23 = (bf16[1,128,256]{2,1,0:T(8,128)(2,1)S(1)}, bf16[1,128,256]{2,1,0:T(8,128)(2,1)S(1)}, u32[]{:S(2)}, u32[]{:S(2)}) collective-permute-start(bf16[1,128,256]{2,1,0:T(8,128)(2,1)S(1)} %get-tuple-element.41), channel_id=1, source_target_pairs={{0,14},{2,12},{4,10},{6,8},{8,6},{10,4},{12,2},{14,0},{1,15},{3,13... | collective-permute-start | bytes 196616 | tf_op jit(solution)/shard_map/ppermute | solution.py:111
  55.7 3.1 %collective-permute-start.20 = (bf16[1,128,256]{2,1,0:T(8,128)(2,1)S(1)}, bf16[1,128,256]{2,1,0:T(8,128)(2,1)S(1)}, u32[]{:S(2)}, u32[]{:S(2)}) collective-permute-start(bf16[1,128,256]{2,1,0:T(8,128)(2,1)S(1)} %get-tuple-element.44), channel_id=1, source_target_pairs={{0,8},{2,10},{4,12},{6,14},{8,0},{10,2},{12,4},{14,6},{1,9},{3,11}... | collective-permute-start | bytes 196616 | tf_op jit(solution)/shard_map/ppermute | solution.py:111
  60.0 3.6 %collective-permute-done.17 = bf16[1,128,256]{2,1,0:T(8,128)(2,1)S(1)} collective-permute-done((bf16[1,128,256]{2,1,0:T(8,128)(2,1)S(1)}, bf16[1,128,256]{2,1,0:T(8,128)(2,1)S(1)}, u32[]{:S(2)}, u32[]{:S(2)}) %collective-permute-start.17) | collective-permute-done | bytes 65568 | tf_op jit(solution)/shard_map/ppermute | solution.py:111
  64.7 3.2 %collective-permute-done.18 = bf16[1,128,256]{2,1,0:T(8,128)(2,1)S(1)} collective-permute-done((bf16[1,128,256]{2,1,0:T(8,128)(2,1)S(1)}, bf16[1,128,256]{2,1,0:T(8,128)(2,1)S(1)}, u32[]{:S(2)}, u32[]{:S(2)}) %collective-permute-start.18) | collective-permute-done | bytes 65568 | tf_op jit(solution)/shard_map/ppermute | solution.py:111
  69.4 3.6 %collective-permute-done.19 = bf16[1,128,256]{2,1,0:T(8,128)(2,1)S(1)} collective-permute-done((bf16[1,128,256]{2,1,0:T(8,128)(2,1)S(1)}, bf16[1,128,256]{2,1,0:T(8,128)(2,1)S(1)}, u32[]{:S(2)}, u32[]{:S(2)}) %collective-permute-start.19) | collective-permute-done | bytes 65568 | tf_op jit(solution)/shard_map/ppermute | solution.py:111
  77.5 2.8 %add_convert_fusion.6 = (bf16[1,8,128,256]{3,2,1,0:T(8,128)(2,1)S(1)}, bf16[1,8,128,256]{3,2,1,0:T(8,128)(2,1)S(1)}, bf16[1,8,128,256]{3,2,1,0:T(8,128)(2,1)S(1)...) fusion(f32[1,8,128,256]{3,1,2,0:T(8,128)S(1)} %bitcast.193, ...), kind=kLoop, calls=%fused_computation.53 | loop fusion | flops 6291456 | bytes 9453568 | tf_op jit(solution)/shard_map/convert.6
  82.9 2.3 %fusion.36 = (bf16[256,256]{1,0:T(8,128)(2,1)S(1)}, bf16[256,256]{1,0:T(8,128)(2,1)S(1)}, bf16[256,256]{1,0:T(8,128)(2,1)S(1)}, bf16[256,256]{1,0:T(8,128)(2,1)S...) fusion(s32[256]{0:T(256)S(1)} %multiply_add_fusion.1), kind=kLoop, calls=%fused_computation.88 | loop fusion | flops 2359296 | bytes 787456 | tf_op jit(solution)/shard_map/convert.15
  102.7 5.2 %all-to-all-start.2 = ((bf16[8,128,256]{2,1,0:T(8,128)(2,1)}), bf16[8,128,256]{2,1,0:T(8,128)(2,1)S(1)}, u32[]{:S(2)}, u32[]{:S(2)}) async-start(bf16[8,128,256]{2,1,0:T(8,128)(2,1)} %copy.100), calls=%async_computation.2 | async-start | bytes 1048576 | tf_op jit(solution)/shard_map/all_to_all | solution.py:137
  109.8 13.1 %all-to-all-done.2 = bf16[8,128,256]{2,1,0:T(8,128)(2,1)S(1)} async-done(((bf16[8,128,256]{2,1,0:T(8,128)(2,1)}), bf16[8,128,256]{2,1,0:T(8,128)(2,1)S(1)}, u32[]{:S(2)}, u32[]{:S(2)}) %all-to-all-start.2) | async-done | bytes 524320 | tf_op jit(solution)/shard_map/all_to_all | solution.py:137
  122.9 3.6 %all-to-all-start = ((bf16[8,128,256]{2,1,0:T(8,128)(2,1)}), bf16[8,128,256]{2,1,0:T(8,128)(2,1)S(1)}, u32[]{:S(2)}, u32[]{:S(2)}) async-start(bf16[8,128,256]{2,1,0:T(8,128)(2,1)} %copy.84), calls=%async_computation | async-start | bytes 1048576 | tf_op jit(solution)/shard_map/all_to_all | solution.py:137
  128.5 12.7 %all-to-all-done = bf16[8,128,256]{2,1,0:T(8,128)(2,1)S(1)} async-done(((bf16[8,128,256]{2,1,0:T(8,128)(2,1)}), bf16[8,128,256]{2,1,0:T(8,128)(2,1)S(1)}, u32[]{:S(2)}, u32[]{:S(2)}) %all-to-all-start) | async-done | bytes 524320 | tf_op jit(solution)/shard_map/all_to_all | solution.py:137
  141.2 3.6 %all-to-all-start.1 = ((bf16[8,128,256]{2,1,0:T(8,128)(2,1)}), bf16[8,128,256]{2,1,0:T(8,128)(2,1)S(1)}, u32[]{:S(2)}, u32[]{:S(2)}) async-start(bf16[8,128,256]{2,1,0:T(8,128)(2,1)} %copy.98), calls=%async_computation.1 | async-start | bytes 1048576 | tf_op jit(solution)/shard_map/all_to_all | solution.py:137
  146.9 12.7 %all-to-all-done.1 = bf16[8,128,256]{2,1,0:T(8,128)(2,1)S(1)} async-done(((bf16[8,128,256]{2,1,0:T(8,128)(2,1)}), bf16[8,128,256]{2,1,0:T(8,128)(2,1)S(1)}, u32[]{:S(2)}, u32[]{:S(2)}) %all-to-all-start.1) | async-done | bytes 524320 | tf_op jit(solution)/shard_map/all_to_all | solution.py:137
  (128 shorter events, 51.5 us)
Async XLA Ops:
  2.8 33.8 %collective-permute-start.14 = (bf16[1,128,256]{2,1,0:T(8,128)(2,1)S(1)}, bf16[1,128,256]{2,1,0:T(8,128)(2,1)}, u32[]{:S(2)}, u32[]{:S(2)}) collective-permute-start(bf16[1,128,256]{2,1,0:T(8,128)(2,1)S(1)} %get-tuple-element.57), channel_id=1, source_target_pairs={{0,14},{2,12},{4,10},{6,8},{8,6},{10,4},{12,2},{14,0},{1,15},{3,13... | collective-permute-start | bytes 196616 | tf_op jit(solution)/shard_map/ppermute | solution.py:111
  8.7 24.6 %collective-permute-start.13 = (bf16[1,128,256]{2,1,0:T(8,128)(2,1)S(1)}, bf16[1,128,256]{2,1,0:T(8,128)(2,1)}, u32[]{:S(2)}, u32[]{:S(2)}) collective-permute-start(bf16[1,128,256]{2,1,0:T(8,128)(2,1)S(1)} %get-tuple-element.58), channel_id=1, source_target_pairs={{0,12},{2,14},{4,8},{6,10},{8,4},{10,6},{12,0},{14,2},{1,13},{3,15... | collective-permute-start | bytes 196616 | tf_op jit(solution)/shard_map/ppermute | solution.py:111
  9.0 22.9 %collective-permute-start.12 = (bf16[1,128,256]{2,1,0:T(8,128)(2,1)S(1)}, bf16[1,128,256]{2,1,0:T(8,128)(2,1)}, u32[]{:S(2)}, u32[]{:S(2)}) collective-permute-start(bf16[1,128,256]{2,1,0:T(8,128)(2,1)S(1)} %get-tuple-element.59), channel_id=1, source_target_pairs={{0,10},{2,8},{4,14},{6,12},{8,2},{10,0},{12,6},{14,4},{1,11},{3,9}... | collective-permute-start | bytes 196616 | tf_op jit(solution)/shard_map/ppermute | solution.py:111
  9.7 21.2 %collective-permute-start.11 = (bf16[1,128,256]{2,1,0:T(8,128)(2,1)S(1)}, bf16[1,128,256]{2,1,0:T(8,128)(2,1)}, u32[]{:S(2)}, u32[]{:S(2)}) collective-permute-start(bf16[1,128,256]{2,1,0:T(8,128)(2,1)S(1)} %get-tuple-element.60), channel_id=1, source_target_pairs={{0,8},{2,10},{4,12},{6,14},{8,0},{10,2},{12,4},{14,6},{1,9},{3,11}... | collective-permute-start | bytes 196616 | tf_op jit(solution)/shard_map/ppermute | solution.py:111
  11.7 4.8 %collective-permute-start.8 = (bf16[1,128,256]{2,1,0:T(8,128)(2,1)}, bf16[1,128,256]{2,1,0:T(8,128)(2,1)}, u32[]{:S(2)}, u32[]{:S(2)}) collective-permute-start(bf16[1,128,256]{2,1,0:T(8,128)(2,1)} %get-tuple-element.63), channel_id=1, source_target_pairs={{0,2},{2,0},{4,6},{6,4},{8,10},{10,8},{12,14},{14,12},{1,3},{3,1},... | collective-permute-start | bytes 196616 | tf_op jit(solution)/shard_map/ppermute | solution.py:111
  16.4 4.5 %collective-permute-start.9 = (bf16[1,128,256]{2,1,0:T(8,128)(2,1)S(1)}, bf16[1,128,256]{2,1,0:T(8,128)(2,1)S(1)}, u32[]{:S(2)}, u32[]{:S(2)}) collective-permute-start(bf16[1,128,256]{2,1,0:T(8,128)(2,1)S(1)} %copy-done.2), channel_id=1, source_target_pairs={{0,4},{2,6},{4,0},{6,2},{8,12},{10,14},{12,8},{14,10},{1,5},{3,7},... | collective-permute-start | bytes 196616 | tf_op jit(solution)/shard_map/ppermute | solution.py:111
  20.9 5.2 %collective-permute-start.10 = (bf16[1,128,256]{2,1,0:T(8,128)(2,1)S(1)}, bf16[1,128,256]{2,1,0:T(8,128)(2,1)S(1)}, u32[]{:S(2)}, u32[]{:S(2)}) collective-permute-start(bf16[1,128,256]{2,1,0:T(8,128)(2,1)S(1)} %get-tuple-element.61), channel_id=1, source_target_pairs={{0,6},{2,4},{4,2},{6,0},{8,14},{10,12},{12,10},{14,8},{1,7},{3,5},... | collective-permute-start | bytes 196616 | tf_op jit(solution)/shard_map/ppermute | solution.py:111
  26.1 32.8 %collective-permute-start.6 = (bf16[1,128,256]{2,1,0:T(8,128)(2,1)S(1)}, bf16[1,128,256]{2,1,0:T(8,128)(2,1)S(1)}, u32[]{:S(2)}, u32[]{:S(2)}) collective-permute-start(bf16[1,128,256]{2,1,0:T(8,128)(2,1)S(1)} %get-tuple-element.49), channel_id=1, source_target_pairs={{0,14},{2,12},{4,10},{6,8},{8,6},{10,4},{12,2},{14,0},{1,15},{3,13... | collective-permute-start | bytes 196616 | tf_op jit(solution)/shard_map/ppermute | solution.py:111
  30.9 24.8 %collective-permute-start.5 = (bf16[1,128,256]{2,1,0:T(8,128)(2,1)S(1)}, bf16[1,128,256]{2,1,0:T(8,128)(2,1)S(1)}, u32[]{:S(2)}, u32[]{:S(2)}) collective-permute-start(bf16[1,128,256]{2,1,0:T(8,128)(2,1)S(1)} %get-tuple-element.50), channel_id=1, source_target_pairs={{0,12},{2,14},{4,8},{6,10},{8,4},{10,6},{12,0},{14,2},{1,13},{3,15... | collective-permute-start | bytes 196616 | tf_op jit(solution)/shard_map/ppermute | solution.py:111
  31.9 23.5 %collective-permute-start.4 = (bf16[1,128,256]{2,1,0:T(8,128)(2,1)S(1)}, bf16[1,128,256]{2,1,0:T(8,128)(2,1)S(1)}, u32[]{:S(2)}, u32[]{:S(2)}) collective-permute-start(bf16[1,128,256]{2,1,0:T(8,128)(2,1)S(1)} %get-tuple-element.51), channel_id=1, source_target_pairs={{0,10},{2,8},{4,14},{6,12},{8,2},{10,0},{12,6},{14,4},{1,11},{3,9}... | collective-permute-start | bytes 196616 | tf_op jit(solution)/shard_map/ppermute | solution.py:111
  33.3 21.9 %collective-permute-start.3 = (bf16[1,128,256]{2,1,0:T(8,128)(2,1)S(1)}, bf16[1,128,256]{2,1,0:T(8,128)(2,1)S(1)}, u32[]{:S(2)}, u32[]{:S(2)}) collective-permute-start(bf16[1,128,256]{2,1,0:T(8,128)(2,1)S(1)} %get-tuple-element.52), channel_id=1, source_target_pairs={{0,8},{2,10},{4,12},{6,14},{8,0},{10,2},{12,4},{14,6},{1,9},{3,11}... | collective-permute-start | bytes 196616 | tf_op jit(solution)/shard_map/ppermute | solution.py:111
  36.6 4.3 %collective-permute-start = (bf16[1,128,256]{2,1,0:T(8,128)(2,1)S(1)}, bf16[1,128,256]{2,1,0:T(8,128)(2,1)S(1)}, u32[]{:S(2)}, u32[]{:S(2)}) collective-permute-start(bf16[1,128,256]{2,1,0:T(8,128)(2,1)S(1)} %get-tuple-element.55), channel_id=1, source_target_pairs={{0,2},{2,0},{4,6},{6,4},{8,10},{10,8},{12,14},{14,12},{1,3},{3,1},... | collective-permute-start | bytes 196616 | tf_op jit(solution)/shard_map/ppermute | solution.py:111
  40.8 4.3 %collective-permute-start.1 = (bf16[1,128,256]{2,1,0:T(8,128)(2,1)S(1)}, bf16[1,128,256]{2,1,0:T(8,128)(2,1)S(1)}, u32[]{:S(2)}, u32[]{:S(2)}) collective-permute-start(bf16[1,128,256]{2,1,0:T(8,128)(2,1)S(1)} %get-tuple-element.54), channel_id=1, source_target_pairs={{0,4},{2,6},{4,0},{6,2},{8,12},{10,14},{12,8},{14,10},{1,5},{3,7},... | collective-permute-start | bytes 196616 | tf_op jit(solution)/shard_map/ppermute | solution.py:111
  45.1 5.9 %collective-permute-start.2 = (bf16[1,128,256]{2,1,0:T(8,128)(2,1)S(1)}, bf16[1,128,256]{2,1,0:T(8,128)(2,1)S(1)}, u32[]{:S(2)}, u32[]{:S(2)}) collective-permute-start(bf16[1,128,256]{2,1,0:T(8,128)(2,1)S(1)} %get-tuple-element.53), channel_id=1, source_target_pairs={{0,6},{2,4},{4,2},{6,0},{8,14},{10,12},{12,10},{14,8},{1,7},{3,5},... | collective-permute-start | bytes 196616 | tf_op jit(solution)/shard_map/ppermute | solution.py:111
  51.0 23.9 %collective-permute-start.23 = (bf16[1,128,256]{2,1,0:T(8,128)(2,1)S(1)}, bf16[1,128,256]{2,1,0:T(8,128)(2,1)S(1)}, u32[]{:S(2)}, u32[]{:S(2)}) collective-permute-start(bf16[1,128,256]{2,1,0:T(8,128)(2,1)S(1)} %get-tuple-element.41), channel_id=1, source_target_pairs={{0,14},{2,12},{4,10},{6,8},{8,6},{10,4},{12,2},{14,0},{1,15},{3,13... | collective-permute-start | bytes 196616 | tf_op jit(solution)/shard_map/ppermute | solution.py:111
  55.3 17.8 %collective-permute-start.22 = (bf16[1,128,256]{2,1,0:T(8,128)(2,1)S(1)}, bf16[1,128,256]{2,1,0:T(8,128)(2,1)S(1)}, u32[]{:S(2)}, u32[]{:S(2)}) collective-permute-start(bf16[1,128,256]{2,1,0:T(8,128)(2,1)S(1)} %get-tuple-element.42), channel_id=1, source_target_pairs={{0,12},{2,14},{4,8},{6,10},{8,4},{10,6},{12,0},{14,2},{1,13},{3,15... | collective-permute-start | bytes 196616 | tf_op jit(solution)/shard_map/ppermute | solution.py:111
  55.4 17.7 %collective-permute-start.21 = (bf16[1,128,256]{2,1,0:T(8,128)(2,1)S(1)}, bf16[1,128,256]{2,1,0:T(8,128)(2,1)S(1)}, u32[]{:S(2)}, u32[]{:S(2)}) collective-permute-start(bf16[1,128,256]{2,1,0:T(8,128)(2,1)S(1)} %get-tuple-element.43), channel_id=1, source_target_pairs={{0,10},{2,8},{4,14},{6,12},{8,2},{10,0},{12,6},{14,4},{1,11},{3,9}... | collective-permute-start | bytes 196616 | tf_op jit(solution)/shard_map/ppermute | solution.py:111
  55.7 17.4 %collective-permute-start.20 = (bf16[1,128,256]{2,1,0:T(8,128)(2,1)S(1)}, bf16[1,128,256]{2,1,0:T(8,128)(2,1)S(1)}, u32[]{:S(2)}, u32[]{:S(2)}) collective-permute-start(bf16[1,128,256]{2,1,0:T(8,128)(2,1)S(1)} %get-tuple-element.44), channel_id=1, source_target_pairs={{0,8},{2,10},{4,12},{6,14},{8,0},{10,2},{12,4},{14,6},{1,9},{3,11}... | collective-permute-start | bytes 196616 | tf_op jit(solution)/shard_map/ppermute | solution.py:111
  58.9 4.8 %collective-permute-start.17 = (bf16[1,128,256]{2,1,0:T(8,128)(2,1)S(1)}, bf16[1,128,256]{2,1,0:T(8,128)(2,1)S(1)}, u32[]{:S(2)}, u32[]{:S(2)}) collective-permute-start(bf16[1,128,256]{2,1,0:T(8,128)(2,1)S(1)} %get-tuple-element.47), channel_id=1, source_target_pairs={{0,2},{2,0},{4,6},{6,4},{8,10},{10,8},{12,14},{14,12},{1,3},{3,1},... | collective-permute-start | bytes 196616 | tf_op jit(solution)/shard_map/ppermute | solution.py:111
  67.9 5.2 %collective-permute-start.19 = (bf16[1,128,256]{2,1,0:T(8,128)(2,1)S(1)}, bf16[1,128,256]{2,1,0:T(8,128)(2,1)S(1)}, u32[]{:S(2)}, u32[]{:S(2)}) collective-permute-start(bf16[1,128,256]{2,1,0:T(8,128)(2,1)S(1)} %get-tuple-element.45), channel_id=1, source_target_pairs={{0,6},{2,4},{4,2},{6,0},{8,14},{10,12},{12,10},{14,8},{1,7},{3,5},... | collective-permute-start | bytes 196616 | tf_op jit(solution)/shard_map/ppermute | solution.py:111
  82.4 4.7 %collective-permute-start.15 = (bf16[2,8,128,256]{3,2,1,0:T(8,128)(2,1)}, bf16[2,8,128,256]{3,2,1,0:T(8,128)(2,1)}, u32[]{:S(2)}, u32[]{:S(2)}) collective-permute-start(bf16[2,8,128,256]{3,2,1,0:T(8,128)(2,1)} %pad_maximum_fusion.1), channel_id=1, source_target_pairs={{0,1},{1,0},{2,3},{3,2},{4,5},{5,4},{6,7},{7,6},{8,9},{9,8},{10,11... | collective-permute-start | bytes 3145736 | tf_op jit(solution)/shard_map/ppermute | solution.py:25
  102.7 20.2 %all-to-all-start.2 = ((bf16[8,128,256]{2,1,0:T(8,128)(2,1)}), bf16[8,128,256]{2,1,0:T(8,128)(2,1)S(1)}, u32[]{:S(2)}, u32[]{:S(2)}) async-start(bf16[8,128,256]{2,1,0:T(8,128)(2,1)} %copy.100), calls=%async_computation.2 | async-start | bytes 1048576 | tf_op jit(solution)/shard_map/all_to_all | solution.py:137
  122.9 18.3 %all-to-all-start = ((bf16[8,128,256]{2,1,0:T(8,128)(2,1)}), bf16[8,128,256]{2,1,0:T(8,128)(2,1)S(1)}, u32[]{:S(2)}, u32[]{:S(2)}) async-start(bf16[8,128,256]{2,1,0:T(8,128)(2,1)} %copy.84), calls=%async_computation | async-start | bytes 1048576 | tf_op jit(solution)/shard_map/all_to_all | solution.py:137
  141.2 18.3 %all-to-all-start.1 = ((bf16[8,128,256]{2,1,0:T(8,128)(2,1)}), bf16[8,128,256]{2,1,0:T(8,128)(2,1)S(1)}, u32[]{:S(2)}, u32[]{:S(2)}) async-start(bf16[8,128,256]{2,1,0:T(8,128)(2,1)} %copy.98), calls=%async_computation.1 | async-start | bytes 1048576 | tf_op jit(solution)/shard_map/all_to_all | solution.py:137
  (9 other events, 49.9 us)
